TPU v7x, 32 devices: a whole 2x2x4 slice. The times are simulated.
32 devices in a mesh: row: 16 (over z, y, core), col: 2 (over x).
Axes of the slice: x: 2, y: 2, z: 4, core: 2. Of those that a mesh axis runs over, the one named last changes fastest.
Arguments:
- p_vals: float32 [64, 4, 128, 128], P('row', 'col'), may hold values from -2 to 2
- p_cols: int32 [64, 4], P('row'), may hold values from 0 to 63, as said below
- out_cols: int32 [64, 4], P('row'), may hold values from 0 to 63, as said below
Outputs:
- c_vals: float32 [64, 4, 128, 128], P('row', 'col')
Inputs may be any that keep to these rules, and one draw needn't show every extreme that they name: Block column indices; p_cols[i, s] // 4 equals (i // 4 + s // 2 - t) mod 16 for some t of 0, 1, 2, 3. `out_cols`: each output block column is p_cols[p_cols[i, s], s2] for some slots s and s2.
All inputs are finite; a program needn't handle non-finite values.
Results may differ from a plain program's by a relative error of at most 0.0003.
Values sent between devices are 32-bit elements; how exact they have to be, the bound alone decides.
No kernel may reach another device: no remote copies, remote signals or barrier semaphores. Data moves between devices by JAX's collectives and lax.ppermute only.
A program may use at most 64 MiB of HBM per device.

v0:
```python
import jax
import jax.numpy as jnp
from jax import lax
from jax.sharding import PartitionSpec as P


def from_behind(block, axis, distance):
    devices = range(lax.axis_size(axis))
    route = [((i - distance) % len(devices), i) for i in devices]
    return lax.ppermute(block, axis, route)


def on_device(p_vals, p_cols, out_cols):
    rows = p_vals.shape[0]
    slots_dev = p_vals.shape[1]
    nrow = lax.axis_size("row")
    ncol = lax.axis_size("col")
    row_at = lax.axis_index("row")
    col_at = lax.axis_index("col")
    own_cols = lax.dynamic_slice_in_dim(p_cols, col_at * slots_dev, slots_dev, 1)
    panel_vals = lax.all_gather(p_vals, "col", axis=1, tiled=True)
    panel_cols = p_cols
    for bit in range((ncol - 1).bit_length()):
        moved = from_behind((panel_vals, panel_cols), "row", nrow - (1 << bit))
        taken = col_at >> bit & 1 == 1
        panel_vals = jnp.where(taken, moved[0], panel_vals)
        panel_cols = jnp.where(taken, moved[1], panel_cols)
    local_ids = jnp.arange(rows, dtype=jnp.int32)

    def contribute(total, vals, cols, step):
        group_now = (row_at + col_at - step) % nrow
        local_k = own_cols - group_now * rows
        select = (local_k[:, :, None] == local_ids[None, None, :]).astype(jnp.float32)
        match = (out_cols[:, :, None, None] == cols[None, None, :, :]).astype(jnp.float32)
        weights = jnp.einsum("isl,iolt->isolt", select, match)
        mixed = jnp.einsum("isolt,ltab->isoab", weights, vals, precision=lax.Precision.HIGHEST)
        return total + jnp.einsum(
            "isab,isobc->ioac", p_vals, mixed, precision=lax.Precision.HIGHEST
        )

    block = p_vals.shape[2]
    total = jnp.zeros((rows, out_cols.shape[1], block, block), jnp.float32)
    near_vals, near_cols = from_behind((panel_vals, panel_cols), "row", 1)
    far_vals, far_cols = from_behind((panel_vals, panel_cols), "row", 2)
    total = contribute(total, panel_vals, panel_cols, 0)
    total = contribute(total, near_vals, near_cols, 1)
    total = contribute(total, far_vals, far_cols, 2)
    return lax.psum_scatter(total, "col", scatter_dimension=1, tiled=True)


def solution(mesh):
    placed = (P("row", "col", None, None), P("row", None), P("row", None))
    return jax.shard_map(
        on_device,
        mesh=mesh,
        in_specs=placed,
        out_specs=P("row", "col", None, None),
        check_vma=False,
    )
```

profile of v0, /device:TPU:1, one launch (start us, length us, event | category | flops | bytes accessed | tf_op | source)
XLA Modules:
  0.0 168.6 jit_solution(17234122712329622436)
XLA Ops:
  6.5 0.0 all-gather.2.cloned.1.call-start
  6.5 0.7 all-gather.2.cloned.1.call-update
  7.3 0.0 all-reduce.3.cloned.1.call-start
  7.3 0.1 collective-permute-start
  7.4 0.8 dynamic-slice_subtract_fusion
  8.2 24.1 %all-gather.2.cloned.1.call-done = f32[4,4,128,128]{3,2,1,0:T(8,128)} async-done(((f32[4,2,128,128]{3,2,1,0:T(8,128)}), f32[4,4,128,128]{3,2,1,0:T(8,128)}) %all-gather.2.cloned.1.call-update) | async-done | bytes 1048592 | tf_op jit(solution)/shard_map/all_gather | solution.py:21
  32.3 0.7 collective-permute-start.1
  33.0 0.0 collective-permute-done
  33.0 0.7 broadcast_select_fusion.1
  33.7 1.2 collective-permute-start.4
  34.9 2.2 %collective-permute-start.2 = (s32[4,4]{1,0:T(4,128)S(1)}, s32[4,4]{1,0:T(4,128)S(1)}, u32[]{:S(2)}, u32[]{:S(2)}) collective-permute-start(s32[4,4]{1,0:T(4,128)S(1)} %broadcast_select_fusion.1), channel_id=1, source_target_pairs={{30,0},{0,2},{2,4},{4,6},{6,8},{8,10},{10,12},{12,14},{14,16},{16,... | collective-permute-start | bytes 200 | tf_op jit(solution)/shard_map/ppermute | solution.py:10
  37.2 1.8 %collective-permute-done.4 = s32[4,4]{1,0:T(4,128)S(1)} collective-permute-done((s32[4,4]{1,0:T(4,128)S(1)}, s32[4,4]{1,0:T(4,128)S(1)}, u32[]{:S(2)}, u32[]{:S(2)}) %collective-permute-start.4) | collective-permute-done | bytes 96 | tf_op jit(solution)/shard_map/ppermute | solution.py:10
  38.9 0.0 collective-permute-done.2
  39.0 0.8 convert_bitcast_fusion
  39.8 0.1 fusion.43
  39.9 6.9 %collective-permute-done.1 = f32[4,4,128,128]{3,2,1,0:T(8,128)S(1)} collective-permute-done((f32[4,4,128,128]{3,2,1,0:T(8,128)}, f32[4,4,128,128]{3,2,1,0:T(8,128)S(1)}, u32[]{:S(2)}, u32[]{:S(2)}) %collective-permute-start.1) | collective-permute-done | bytes 1048608 | tf_op jit(solution)/shard_map/ppermute | solution.py:10
  46.8 2.3 %broadcast_select_fusion = f32[4,4,128,128]{3,2,1,0:T(8,128)} fusion(f32[4,4,128,128]{3,2,1,0:T(8,128)S(1)} %collective-permute-done.1, f32[4,4,128,128]{3,2,1,0:T(8,128)} %all-gather.2.cloned.1.call-done, pred[]{:T(512)S(6)} %eq.39), kind=kLoop, calls=%fused_computation.21 | loop fusion | flops 262144 | bytes 3145729 | tf_op jit(solution)/shard_map/jit(_where)/select_n | solution.py:26
  49.1 0.0 collective-permute-start.3
  49.1 0.1 fusion.41
  49.3 0.1 fusion.39
  49.4 2.1 %collective-permute-start.5 = (f32[4,4,128,128]{3,2,1,0:T(8,128)}, f32[4,4,128,128]{3,2,1,0:T(8,128)}, u32[]{:S(2)}, u32[]{:S(2)}) collective-permute-start(f32[4,4,128,128]{3,2,1,0:T(8,128)} %broadcast_select_fusion), channel_id=1, source_target_pairs={{28,0},{30,2},{0,4},{2,6},{4,8},{6,10},{8,12},{10,14},{12,16},{14,... | collective-permute-start | bytes 3145736 | tf_op jit(solution)/shard_map/ppermute | solution.py:10
  51.5 15.9 %fusion.28 = f32[4,2,4,128,128,1]{4,1,5,3,2,0:T(2,128)} fusion(f32[4,4,128,128,1,1]{3,2,1,0,4,5:T(8,128)} %bitcast.4, f32[4,2,4,4,4,1]{1,4,3,5,2,0:T(4,128)S(1)} %fusion.43), kind=kOutput, calls=%fused_computation.16 | convolution fusion | flops 100663296 | bytes 3147776 | tf_op jit(solution)/shard_map/isolt,ltab->isoab/dot_general | solution.py:36
  67.4 0.0 copy-start
  67.4 2.8 %copy.14 = f32[4,2,4,128,128,1]{3,4,1,2,0,5:T(8,128)S(1)} copy(f32[4,2,4,128,128,1]{4,1,5,3,2,0:T(2,128)} %fusion.28) | data formatting | bytes 4194304 | tf_op jit(solution)/shard_map/isolt,ltab->isoab/dot_general | solution.py:36
  70.2 0.0 copy-done
  70.2 2.9 %fusion.6 = f32[4,4,128,128]{3,2,1,0:T(8,128)} fusion(f32[4,2,4,128,128,1]{3,4,1,2,0,5:T(8,128)S(1)} %copy.14, f32[4,2,128,128]{3,2,1,0:T(8,128)S(1)} %copy-done), kind=kOutput, calls=%fused_computation.6 | convolution fusion | flops 805306368 | bytes 3670016 | tf_op jit(solution)/shard_map/isab,isobc->ioac/dot_general | solution.py:37
  73.1 0.0 collective-permute-done.3
  73.1 15.8 %fusion.26 = f32[4,2,4,128,128,1]{4,1,5,3,2,0:T(2,128)} fusion(f32[4,4,128,128,1,1]{3,2,1,0,4,5:T(8,128)} %bitcast.14, f32[4,2,4,4,4,1]{1,4,3,5,2,0:T(4,128)S(1)} %fusion.41), kind=kOutput, calls=%fused_computation.14 | convolution fusion | flops 100663296 | bytes 3147776 | tf_op jit(solution)/shard_map/isolt,ltab->isoab/dot_general | solution.py:36
  89.0 2.7 %copy.19 = f32[4,2,4,128,128,1]{3,4,1,2,0,5:T(8,128)S(1)} copy(f32[4,2,4,128,128,1]{4,1,5,3,2,0:T(2,128)} %fusion.26) | data formatting | bytes 4194304 | tf_op jit(solution)/shard_map/isolt,ltab->isoab/dot_general | solution.py:36
  91.7 0.0 collective-permute-done.5
  91.7 16.1 %fusion.24 = f32[4,2,4,128,128,1]{4,1,5,3,2,0:T(2,128)} fusion(f32[4,4,128,128,1,1]{3,2,1,0,4,5:T(8,128)} %bitcast.23, f32[4,2,4,4,4,1]{1,4,3,5,2,0:T(4,128)S(1)} %fusion.39), kind=kOutput, calls=%fused_computation.12 | convolution fusion | flops 100663296 | bytes 3147776 | tf_op jit(solution)/shard_map/isolt,ltab->isoab/dot_general | solution.py:36
  107.8 4.1 %copy.23 = f32[4,2,4,128,128,1]{3,4,1,2,0,5:T(8,128)} copy(f32[4,2,4,128,128,1]{4,1,5,3,2,0:T(2,128)} %fusion.24) | data formatting | bytes 4194304 | tf_op jit(solution)/shard_map/isolt,ltab->isoab/dot_general | solution.py:36
  111.9 0.0 copy-start.1
  111.9 3.3 %fusion.21 = f32[4,4,128,128]{3,2,1,0:T(8,128)S(1)} fusion(f32[4,4,128,128]{3,2,1,0:T(8,128)} %fusion.6, f32[4,2,4,128,128,1]{3,4,1,2,0,5:T(8,128)S(1)} %copy.19, f32[4,2,128,128]{3,2,1,0:T(8,128)S(1)} %copy-done), kind=kOutput, calls=%fused_computation.11 | convolution fusion | flops 805568512 | bytes 4718592 | tf_op jit(solution)/shard_map/isab,isobc->ioac/dot_general | solution.py:37
  115.3 0.0 copy-done.1
  115.3 0.0 copy-start.2
  115.3 2.9 %fusion.18 = f32[4,4,128,128]{2,3,1,0:T(8,128)} fusion(f32[4,4,128,128]{3,2,1,0:T(8,128)S(1)} %fusion.21, f32[4,2,4,128,128,1]{3,4,1,2,0,5:T(8,128)S(1)} %copy-done.1, f32[4,2,128,128]{3,2,1,0:T(8,128)S(1)} %copy-done), kind=kOutput, calls=%fused_computation.10 | convolution fusion | flops 805568512 | bytes 4718592 | tf_op jit(solution)/shard_map/isab,isobc->ioac/dot_general | solution.py:37
  118.2 0.0 all-reduce.3.cloned.1.call-update
  118.3 0.0 copy-done.2
  118.3 0.6 dynamic-slice
  119.5 40.2 %all-reduce.3.cloned.1.call-done = f32[4,4,128,128]{2,3,1,0:T(8,128)} async-done(((f32[4,4,128,128]{2,3,1,0:T(8,128)}), f32[4,4,128,128]{2,3,1,0:T(8,128)}) %all-reduce.3.cloned.1.call-update) | async-done | bytes 1048592
  159.7 1.1 constant_dynamic-slice_fusion
  160.8 1.0 copy.11
  (6 shorter events, 0.0 us)
Async XLA Ops:
  6.5 25.8 %all-gather.2.cloned.1.call-start = ((), (), s32[]{:S(2)}) async-start(), calls=%async_computation | async-start | bytes 1572864 | tf_op jit(solution)/shard_map/all_gather | solution.py:21
  7.3 152.4 %all-reduce.3.cloned.1.call-start = ((), (), s32[]{:S(2)}) async-start(), calls=%async_computation.1 | async-start | bytes 2097152
  7.3 25.7 %collective-permute-start = (s32[4,4]{1,0:T(4,128)}, s32[4,4]{1,0:T(4,128)S(1)}, u32[]{:S(2)}, u32[]{:S(2)}) collective-permute-start(s32[4,4]{1,0:T(4,128)} %param.4), channel_id=1, source_target_pairs={{2,0},{4,2},{6,4},{8,6},{10,8},{12,10},{14,12},{16,14},{18,16},{20... | collective-permute-start | bytes 200 | tf_op jit(solution)/shard_map/ppermute | solution.py:10
  32.3 14.5 %collective-permute-start.1 = (f32[4,4,128,128]{3,2,1,0:T(8,128)}, f32[4,4,128,128]{3,2,1,0:T(8,128)S(1)}, u32[]{:S(2)}, u32[]{:S(2)}) collective-permute-start(f32[4,4,128,128]{3,2,1,0:T(8,128)} %all-gather.2.cloned.1.call-done), channel_id=1, source_target_pairs={{2,0},{4,2},{6,4},{8,6},{10,8},{12,10},{14,12},{16,14},{18,16},{20... | collective-permute-start | bytes 3145736 | tf_op jit(solution)/shard_map/ppermute | solution.py:10
  33.7 5.2 %collective-permute-start.4 = (s32[4,4]{1,0:T(4,128)S(1)}, s32[4,4]{1,0:T(4,128)S(1)}, u32[]{:S(2)}, u32[]{:S(2)}) collective-permute-start(s32[4,4]{1,0:T(4,128)S(1)} %broadcast_select_fusion.1), channel_id=1, source_target_pairs={{28,0},{30,2},{0,4},{2,6},{4,8},{6,10},{8,12},{10,14},{12,16},{14,... | collective-permute-start | bytes 200 | tf_op jit(solution)/shard_map/ppermute | solution.py:10
  34.9 4.0 %collective-permute-start.2 = (s32[4,4]{1,0:T(4,128)S(1)}, s32[4,4]{1,0:T(4,128)S(1)}, u32[]{:S(2)}, u32[]{:S(2)}) collective-permute-start(s32[4,4]{1,0:T(4,128)S(1)} %broadcast_select_fusion.1), channel_id=1, source_target_pairs={{30,0},{0,2},{2,4},{4,6},{6,8},{8,10},{10,12},{12,14},{14,16},{16,... | collective-permute-start | bytes 200 | tf_op jit(solution)/shard_map/ppermute | solution.py:10
  49.1 24.0 %collective-permute-start.3 = (f32[4,4,128,128]{3,2,1,0:T(8,128)}, f32[4,4,128,128]{3,2,1,0:T(8,128)}, u32[]{:S(2)}, u32[]{:S(2)}) collective-permute-start(f32[4,4,128,128]{3,2,1,0:T(8,128)} %broadcast_select_fusion), channel_id=1, source_target_pairs={{30,0},{0,2},{2,4},{4,6},{6,8},{8,10},{10,12},{12,14},{14,16},{16,... | collective-permute-start | bytes 3145736 | tf_op jit(solution)/shard_map/ppermute | solution.py:10
  49.4 42.3 %collective-permute-start.5 = (f32[4,4,128,128]{3,2,1,0:T(8,128)}, f32[4,4,128,128]{3,2,1,0:T(8,128)}, u32[]{:S(2)}, u32[]{:S(2)}) collective-permute-start(f32[4,4,128,128]{3,2,1,0:T(8,128)} %broadcast_select_fusion), channel_id=1, source_target_pairs={{28,0},{30,2},{0,4},{2,6},{4,8},{6,10},{8,12},{10,14},{12,16},{14,... | collective-permute-start | bytes 3145736 | tf_op jit(solution)/shard_map/ppermute | solution.py:10
  67.4 2.8 %copy-start = (f32[4,2,128,128]{3,2,1,0:T(8,128)S(1)}, f32[4,2,128,128]{3,2,1,0:T(8,128)}, u32[]{:S(2)}) copy-start(f32[4,2,128,128]{3,2,1,0:T(8,128)} %param.3) | copy-start | bytes 1572868
  111.9 3.4 %copy-start.1 = (f32[4,2,4,128,128,1]{3,4,1,2,0,5:T(8,128)S(1)}, f32[4,2,4,128,128,1]{3,4,1,2,0,5:T(8,128)}, u32[]{:S(2)}) copy-start(f32[4,2,4,128,128,1]{3,4,1,2,0,5:T(8,128)} %copy.23) | copy-start | bytes 6291460
  115.3 3.0 %copy-start.2 = (u32[32]{0:T(128)S(1)}, u32[32]{0:T(128)}, u32[]{:S(2)}) copy-start(u32[32]{0:T(128)} %constant.45) | copy-start | bytes 388
Sparse Core Ops, SparseCore 0:
  8.9 23.3 all-gather.1
  118.4 41.2 all-reduce.2
where the time goes:
time: 170 us; the launch traced here: 169 us
  waiting for transfers between devices  73.7 us (43%)
  matrix products  57 us (34%)
  between operations  14.2 us (8%)
  local copies, waits for them, and re-layouts  12.3 us (7%)
  starting transfers between devices  6.38 us (4%)
  other arithmetic  4.94 us (3%)
    dot_general x3, matrix products, contribute(): jnp.einsum('isolt,ltab->isoab', weights, vals, precision=lax.Precision.HI...  47.8 us
    unnamed x3, waiting for transfers between devices  40.9 us
    all_gather x1, waiting for transfers between devices, on_device(): panel_vals = lax.all_gather(p_vals, 'col', axis=1, tiled=True)  24.1 us
    dot_general x3, local copies, waits for them, and re-layouts, contribute(): jnp.einsum('isolt,ltab->isoab', weights, vals, precision=lax.Precision.HI...  9.63 us
    dot_general x3, matrix products, contribute(): jnp.einsum('isab,isobc->ioac', p_vals, mixed, precision=lax.Precision.HIG...  9.18 us
    ppermute x6, waiting for transfers between devices, from_behind(): return lax.ppermute(block, axis, route)  8.72 us
    ppermute x6, starting transfers between devices, from_behind(): return lax.ppermute(block, axis, route)  6.34 us
  transfers between devices with their start and end apart: 8, of which 4 were waited for; matrix products, arithmetic and copies ran while one was open for 26% of the time, Pallas kernels for 0%

commit v1 on v0

v1 whole, which is shorter than its diff:
```python
import functools

import jax
import jax.numpy as jnp
from jax import lax
from jax.experimental import pallas as pl
from jax.experimental.pallas import tpu as pltpu
from jax.sharding import PartitionSpec as P

WINDOW = 3
HBM = pl.BlockSpec(memory_space=pltpu.HBM)
SMEM = pl.BlockSpec(memory_space=pltpu.SMEM)


def split(x):
    high = x.astype(jnp.bfloat16)
    return high, (x - high.astype(jnp.float32)).astype(jnp.bfloat16)


def product_kernel(n_left, layers, has_total, *refs):
    refs = list(refs)
    place, weight = refs.pop(0), refs.pop(0)
    left_hbm = [refs.pop(0) for _ in range(n_left)]
    right_hbm = [[refs.pop(0) for _ in range(n)] for n in layers]
    total_hbm = refs.pop(0) if has_total else None
    out_ref = refs.pop(0)
    left = refs.pop(0)
    right = [refs.pop(0) for _ in layers]
    total = refs.pop(0) if has_total else None
    high, low, sems = refs
    rows, slots, block = left.shape[0], left.shape[1], left.shape[3]
    slots_dev = slots // n_left
    outs = out_ref.shape[1]

    copies = []

    def bring(source, target):
        copy = pltpu.make_async_copy(source, target, sems.at[len(copies)])
        copy.start()
        copies.append(copy)

    for at, source in enumerate(left_hbm):
        bring(source, left.at[:, pl.ds(at * slots_dev, slots_dev)])
    for sources, target in zip(right_hbm, right):
        for at, source in enumerate(sources):
            bring(source, target.at[pl.ds(at * rows, rows)])
    if has_total:
        bring(total_hbm, total)
    for copy in copies:
        copy.wait()

    def one_row(i, carry):
        for s in range(slots):
            mixed = [jnp.zeros((block, block), jnp.float32) for _ in range(outs)]
            for layer in range(len(layers)):
                at = (layer * rows + i) * slots + s
                row = place[at]
                for t in range(slots_dev):
                    tile = right[layer][row, t]
                    for o in range(outs):
                        mixed[o] += weight[(at * slots_dev + t) * outs + o] * tile
            for o in range(outs):
                here = (pl.ds(s * block, block), pl.ds(o * block, block))
                high[here], low[here] = split(mixed[o])
        left_high, left_low = split(jnp.concatenate([left[i, s] for s in range(slots)], axis=1))
        dot = functools.partial(jnp.dot, preferred_element_type=jnp.float32)
        result = dot(left_high, high[...]) + (dot(left_high, low[...]) + dot(left_low, high[...]))
        for o in range(outs):
            piece = result[:, o * block:(o + 1) * block]
            out_ref[i, o] = piece + total[i, o] if has_total else piece
        return carry

    lax.fori_loop(0, rows, one_row, 0)


def add_products(place, weight, left, layers, total):
    rows, slots_dev, block = left[0].shape[:3]
    slots = len(left) * slots_dev
    sizes = tuple(len(layer) for layer in layers)
    operands = [*left, *(x for layer in layers for x in layer)] + ([] if total is None else [total])
    shape = jax.ShapeDtypeStruct(left[0].shape, jnp.float32)
    scratch = [pltpu.VMEM((rows, slots, block, block), jnp.float32)]
    scratch += [pltpu.VMEM((n * rows, slots_dev, block, block), jnp.float32) for n in sizes]
    if total is not None:
        scratch.append(pltpu.VMEM(shape.shape, jnp.float32))
    scratch += [pltpu.VMEM((slots * block, slots_dev * block), jnp.bfloat16)] * 2
    scratch.append(pltpu.SemaphoreType.DMA((len(operands),)))
    flops = 2 * rows * slots * slots_dev * block**3 * 3
    return pl.pallas_call(
        functools.partial(product_kernel, len(left), sizes, total is not None),
        out_shape=shape,
        in_specs=[SMEM, SMEM] + [HBM] * len(operands),
        out_specs=pl.BlockSpec(memory_space=pltpu.VMEM),
        scratch_shapes=scratch,
        compiler_params=pltpu.CompilerParams(vmem_limit_bytes=48 * 2**20),
        cost_estimate=pl.CostEstimate(flops=flops, bytes_accessed=4 * left[0].size * (len(operands) + 1), transcendentals=0),
    )(jnp.concatenate([x.reshape(-1) for x in place]), jnp.concatenate([x.reshape(-1) for x in weight]), *operands)


def on_device(p_vals, p_cols, out_cols):
    rows, slots_dev = p_vals.shape[:2]
    slots, outs_dev = p_cols.shape[1], out_cols.shape[1] // lax.axis_size("col")
    nrow, ncol = lax.axis_size("row"), lax.axis_size("col")
    row_at, col_at = lax.axis_index("row"), lax.axis_index("col")

    def permute(x, source):
        pairs = []
        for r in range(nrow):
            for c in range(ncol):
                if source(r, c) is not None:
                    from_row, from_col = source(r, c)
                    pairs.append((from_row % nrow * ncol + from_col % ncol, r * ncol + c))
        return lax.ppermute(x, ("row", "col"), pairs)

    ring = jnp.concatenate([p_cols, p_cols], axis=1)
    cols_here = lax.dynamic_slice_in_dim(ring, col_at * slots_dev, slots, 1)
    halves = (col_at + jnp.arange(slots, dtype=jnp.int32) // slots_dev) % ncol
    group = cols_here // rows
    live = (row_at + halves[None, :] - group) % nrow < WINDOW
    outs_here = lax.dynamic_slice_in_dim(out_cols, col_at * outs_dev, outs_dev, 1)
    cols_at = {d: permute(p_cols, lambda r, c, d=d: (r + d, c)) for d in range(1 - WINDOW, ncol) if d}
    cols_at[0] = p_cols

    def weights(offsets, tables, half):
        found = (group[:, :, None] - row_at - jnp.stack(offsets)) % nrow == 0
        inside = jnp.any(found, axis=2)
        position = jnp.sum(jnp.where(found, jnp.arange(len(offsets), dtype=jnp.int32), 0), axis=2)
        place = jnp.where(inside, position * rows + cols_here % rows, 0)
        table = lax.dynamic_slice_in_dim(jnp.concatenate(tables, axis=0), half * slots_dev, slots_dev, 1)
        chosen = place[:, :, None] == jnp.arange(table.shape[0], dtype=jnp.int32)
        inner = jnp.sum(jnp.where(chosen[:, :, :, None], table[None, None], 0), axis=2)
        match = inner[:, :, :, None] == outs_here[:, None, None, :]
        return place, (match & (live & inside)[:, :, None, None]).astype(jnp.float32)

    if ncol == 2 and nrow % 2 == 0:
        even = row_at % 2 == 0

        def by_core(from_even, from_odd):
            return lambda r, c: (from_odd if r % 2 else from_even)(r, c)

        def across(r, c):
            return r, c + 1

        def behind(r, c):
            return r - 2, c

        def ahead(r, c):
            return r + 2, c

        def beside(r, c):
            return r ^ 1, c

        def none(r, c):
            return None

        first = permute(p_vals, by_core(across, behind))
        second = permute(p_vals, by_core(behind, across))
        beside_own = permute(p_vals, beside)
        third = permute(first, by_core(ahead, across))
        late_own, _ = lax.optimization_barrier((p_vals, first))
        fifth = permute(late_own, by_core(none, lambda r, c: (r + 1, c)))
        fourth = permute(second, by_core(across, none))
        beside_first = permute(first, beside)
        beside_second = permute(second, by_core(beside, none))
        beside_third = permute(third, beside)

        def pick(x, y):
            return jnp.where(even, x, y)

        other = pick(first, second)
        near, far = pick(1, -1), pick(-1, 1)
        near_cols, far_cols = pick(cols_at[1], cols_at[-1]), pick(cols_at[-1], cols_at[1])
        back = jnp.int32(-2)
        zero = jnp.int32(0)
        mate = (col_at + 1) % ncol
        place_c, weight_c = weights([zero, near, back, far], [p_cols, near_cols, cols_at[-2], far_cols], col_at)
        place_n, weight_n = weights([zero, near], [p_cols, near_cols], mate)
        place_l, weight_l = weights([back, far], [cols_at[-2], far_cols], mate)
        left = [p_vals, other]
        total = add_products(
            [place_c, place_n],
            [weight_c, weight_n],
            left,
            [
                [p_vals, beside_own, pick(second, first), pick(beside_first, fifth)],
                [other, pick(beside_second, beside_first)],
            ],
            None,
        )
        return add_products([place_l], [weight_l], left, [[pick(fourth, third), beside_third]], total)

    left = [p_vals] + [permute(p_vals, lambda r, c, j=j: (r, c + j)) for j in range(1, ncol)]
    offsets = list(range(1 - WINDOW, ncol))
    shards = [p_vals if d == 0 else permute(p_vals, lambda r, c, d=d: (r + d, c)) for d in offsets]
    total = None
    for j in range(ncol):
        layer = shards if j == 0 else [permute(x, lambda r, c, j=j: (r, c + j)) for x in shards]
        tables = [cols_at[d] for d in offsets]
        place, weight = weights([jnp.int32(d) for d in offsets], tables, (col_at + j) % ncol)
        total = add_products([place], [weight], left, [layer], total)
    return total


def solution(mesh):
    placed = (P("row", "col", None, None), P("row", None), P("row", None))
    return jax.shard_map(
        on_device,
        mesh=mesh,
        in_specs=placed,
        out_specs=P("row", "col", None, None),
        check_vma=False,
    )
```

time: 170 us -> 42.2 us (0.25)
  the two profiles are of different devices: /device:TPU:1 before, /device:TPU:0 now
where the time goes in v1:
time: 42.2 us; the launch traced here: 41.9 us
  starting transfers between devices  17.4 us (41%)
  waiting for transfers between devices  12.2 us (29%)
  Pallas kernels  5.89 us (14%)
  other arithmetic  3.76 us (9%)
  local copies, waits for them, and re-layouts  2.48 us (6%)
    ppermute x12, starting transfers between devices, permute(): return lax.ppermute(x, ('row', 'col'), pairs)  17.4 us
    ppermute x12, waiting for transfers between devices, permute(): return lax.ppermute(x, ('row', 'col'), pairs)  12.2 us
    pallas_call x2, Pallas kernels, add_products(): pl.pallas_call(functools.partial(product_kernel, len(left), sizes, total...  5.89 us
    unnamed x7, local copies, waits for them, and re-layouts  1.46 us
    select_n x4, other arithmetic, pick(): return jnp.where(even, x, y)  1.31 us
  transfers between devices with their start and end apart: 12, of which 5 were waited for; matrix products, arithmetic and copies ran while one was open for 13% of the time, Pallas kernels for 7%

profile of v1, /device:TPU:0, one launch (start us, length us, event | category | flops | bytes accessed | tf_op | source)
XLA Modules:
  0.0 41.9 jit_solution(12256627393409521390)
XLA Ops:
  0.0 2.9 %collective-permute-start.3 = (f32[4,2,128,128]{3,2,1,0:T(8,128)}, f32[4,2,128,128]{3,2,1,0:T(8,128)S(1)}, u32[]{:S(2)}, u32[]{:S(2)}) collective-permute-start(f32[4,2,128,128]{3,2,1,0:T(8,128)} %refs_2_.3), channel_id=1, source_target_pairs={{1,0},{0,1},{30,2},{31,3},{5,4},{4,5},{2,6},{3,7},{9,8},{8,9},{6,1... | collective-permute-start | bytes 1572872 | tf_op jit(solution)/shard_map/ppermute | solution.py:113
  2.9 1.5 %collective-permute-start.4 = (f32[4,2,128,128]{3,2,1,0:T(8,128)}, f32[4,2,128,128]{3,2,1,0:T(8,128)S(1)}, u32[]{:S(2)}, u32[]{:S(2)}) collective-permute-start(f32[4,2,128,128]{3,2,1,0:T(8,128)} %refs_2_.3), channel_id=1, source_target_pairs={{28,0},{29,1},{3,2},{2,3},{0,4},{1,5},{7,6},{6,7},{4,8},{5,9},{11,... | collective-permute-start | bytes 1572872 | tf_op jit(solution)/shard_map/ppermute | solution.py:113
  4.5 0.8 %copy.12 = s32[4,4]{0,1:T(4,128)S(1)} copy(s32[4,4]{1,0:T(4,128)} %param.4) | data formatting | bytes 128 | tf_op args[1]
  5.2 4.4 %collective-permute-start.2 = (s32[4,4]{0,1:T(4,128)S(1)}, s32[4,4]{0,1:T(4,128)S(1)}, u32[]{:S(2)}, u32[]{:S(2)}) collective-permute-start(s32[4,4]{0,1:T(4,128)S(1)} %copy.12), channel_id=1, source_target_pairs={{2,0},{3,1},{4,2},{5,3},{6,4},{7,5},{8,6},{9,7},{10,8},{11,9},{12,... | collective-permute-start | bytes 200 | tf_op jit(solution)/shard_map/ppermute | solution.py:113
  9.7 0.7 %copy-done.2 = s32[4,4]{1,0:T(4,128)S(1)} copy-done((s32[4,4]{1,0:T(4,128)S(1)}, s32[4,4]{1,0:T(4,128)}, u32[]{:S(2)}) %copy-start.2) | copy-done | bytes 88
  10.4 0.1 pad_add_fusion
  10.4 0.1 pad_add_fusion.4
  10.5 0.1 fusion.10
  10.6 0.1 broadcast_subtract_fusion
  10.7 0.2 select_reduce_fusion.3
  10.9 0.2 fusion.12
  11.1 0.1 select_reduce_fusion.4
  11.3 0.1 add_select_fusion.7
  11.3 0.1 iota_compare_fusion.1
  11.4 0.1 reshape.88
  11.5 0.1 iota_compare_fusion
  11.6 0.1 reshape.89
  11.7 0.1 iota_compare_fusion.2
  11.7 0.1 reshape.87.refs_0_
  11.9 0.1 constant_dynamic-slice_fusion.2
  11.9 0.1 pad_add_fusion.7.refs_0_
  12.0 3.6 %collective-permute-done.1 = s32[4,4]{0,1:T(4,128)S(1)} collective-permute-done((s32[4,4]{0,1:T(4,128)S(1)}, s32[4,4]{0,1:T(4,128)S(1)}, u32[]{:S(2)}, u32[]{:S(2)}) %collective-permute-start.1) | collective-permute-done | bytes 96 | tf_op jit(solution)/shard_map/ppermute | solution.py:113
  15.6 2.6 %collective-permute-done = s32[4,4]{0,1:T(4,128)S(1)} collective-permute-done((s32[4,4]{0,1:T(4,128)S(1)}, s32[4,4]{0,1:T(4,128)S(1)}, u32[]{:S(2)}, u32[]{:S(2)}) %collective-permute-start) | collective-permute-done | bytes 96 | tf_op jit(solution)/shard_map/ppermute | solution.py:113
  18.2 0.1 pad_add_fusion.1
  18.3 0.2 select_reduce_fusion.2
  18.5 0.1 copy.15
  18.7 0.1 pad_add_fusion.3
  18.7 0.2 select_reduce_fusion
  19.0 0.1 copy.19
  19.1 0.1 pad_add_fusion.2
  19.2 1.3 %collective-permute-start.10 = (f32[4,2,128,128]{3,2,1,0:T(8,128)}, f32[4,2,128,128]{3,2,1,0:T(8,128)S(1)}, u32[]{:S(2)}, u32[]{:S(2)}) collective-permute-start(f32[4,2,128,128]{3,2,1,0:T(8,128)} %refs_2_.3), channel_id=1, source_target_pairs={{4,2},{5,3},{8,6},{9,7},{12,10},{13,11},{16,14},{17,15},{20,18},{2... | collective-permute-start | bytes 1572872 | tf_op jit(solution)/shard_map/ppermute | solution.py:113
  20.5 0.2 select_reduce_fusion.1
  20.7 0.1 copy.17
  20.9 1.8 %collective-permute-start.6 = (f32[4,2,128,128]{3,2,1,0:T(8,128)S(1)}, f32[4,2,128,128]{3,2,1,0:T(8,128)S(1)}, u32[]{:S(2)}, u32[]{:S(2)}) collective-permute-start(f32[4,2,128,128]{3,2,1,0:T(8,128)S(1)} %collective-permute-done.3), channel_id=1, source_target_pairs={{4,0},{5,1},{3,2},{2,3},{8,4},{9,5},{7,6},{6,7},{12,8},{13,9},{11,... | collective-permute-start | bytes 1572872 | tf_op jit(solution)/shard_map/ppermute | solution.py:113
  22.7 1.3 %collective-permute-start.11 = (f32[4,2,128,128]{3,2,1,0:T(8,128)S(1)}, f32[4,2,128,128]{3,2,1,0:T(8,128)}, u32[]{:S(2)}, u32[]{:S(2)}) collective-permute-start(f32[4,2,128,128]{3,2,1,0:T(8,128)S(1)} %collective-permute-done.4), channel_id=1, source_target_pairs={{2,0},{3,1},{6,4},{7,5},{10,8},{11,9},{14,12},{15,13},{18,16},{19,... | collective-permute-start | bytes 1572872 | tf_op jit(solution)/shard_map/ppermute | solution.py:113
  23.9 0.2 compare_and_fusion.1
  24.1 0.1 convert_element_type.19
  24.2 0.1 convert_element_type.20
  24.3 0.1 reshape.90.refs_1_
  24.5 0.1 add_convert_fusion.refs_1_
  24.5 2.9 %collective-permute-done.10 = f32[4,2,128,128]{3,2,1,0:T(8,128)S(1)} collective-permute-done((f32[4,2,128,128]{3,2,1,0:T(8,128)}, f32[4,2,128,128]{3,2,1,0:T(8,128)S(1)}, u32[]{:S(2)}, u32[]{:S(2)}) %collective-permute-start.10) | collective-permute-done | bytes 524320 | tf_op jit(solution)/shard_map/ppermute | solution.py:113
  27.5 4.1 %collective-permute-start.5 = (f32[4,2,128,128]{3,2,1,0:T(8,128)S(1)}, f32[4,2,128,128]{3,2,1,0:T(8,128)S(1)}, u32[]{:S(2)}, u32[]{:S(2)}) collective-permute-start(f32[4,2,128,128]{3,2,1,0:T(8,128)S(1)} %collective-permute-done.4), channel_id=1, source_target_pairs={{1,0},{0,1},{5,4},{4,5},{9,8},{8,9},{13,12},{12,13},{17,16},{16,17... | collective-permute-start | bytes 1572872 | tf_op jit(solution)/shard_map/ppermute | solution.py:113
  31.6 0.1 broadcast_select_fusion.2
  31.7 1.9 %collective-permute-done.6 = f32[4,2,128,128]{3,2,1,0:T(8,128)S(1)} collective-permute-done((f32[4,2,128,128]{3,2,1,0:T(8,128)S(1)}, f32[4,2,128,128]{3,2,1,0:T(8,128)S(1)}, u32[]{:S(2)}, u32[]{:S(2)}) %collective-permute-start.6) | collective-permute-done | bytes 524320 | tf_op jit(solution)/shard_map/ppermute | solution.py:113
  33.6 1.1 %broadcast_select_fusion = (f32[4,2,128,128]{3,2,1,0:T(8,128)S(1)}, f32[4,2,128,128]{3,2,1,0:T(8,128)S(1)}) fusion(f32[4,2,128,128]{3,2,1,0:T(8,128)} %collective-permute-done.11, f32[4,2,128,128]{3,2,1,0:T(8,128)S(1)} %collective-permute-done.9, pred[]{:T(512)S(6)} %eq.120, f32[4,2,128,128]{3,2,1,0:T(8,128)S(1)} %collective-permute-done.10), kind=kLoop, calls=%fused_computation | loop fusion | flops 262144 | bytes 2621441 | tf_op jit(solution)/shard_map/jit(_where)/select_n | solution.py:168
  34.8 2.8 %shard_map.37.refs_6_ = f32[4,2,128,128]{3,2,1,0:T(8,128)S(1)} custom-call(s32[32]{0:T(128)S(1)} %pad_add_fusion.7.refs_0_, f32[128]{0:T(128)S(1)} %add_convert_fusion.refs_1_, f32[4,2,128,128]{3,2,1,0:T(8,128)S(1)} %copy-done.1, f32[4,2,128,128]{3,2,1,0:T(8,128)S(1)} %get-tuple-element.16.refs_3_.refs_8_, f32[4,2,128,128]{3,2,1,0:T(8,128)S(1)} %copy-done.1, ...), custom_call_target="tpu_custom_call" | custom-call | flops 402653184 | bytes 4718592 | tf_op jit(solution)/shard_map/pallas_call | solution.py:89
  37.6 1.2 %collective-permute-done.5 = f32[4,2,128,128]{3,2,1,0:T(8,128)S(1)} collective-permute-done((f32[4,2,128,128]{3,2,1,0:T(8,128)S(1)}, f32[4,2,128,128]{3,2,1,0:T(8,128)S(1)}, u32[]{:S(2)}, u32[]{:S(2)}) %collective-permute-start.5) | collective-permute-done | bytes 524320 | tf_op jit(solution)/shard_map/ppermute | solution.py:113
  38.8 3.1 %shard_map.38 = f32[4,2,128,128]{3,2,1,0:T(8,128)} custom-call(s32[16]{0:T(128)S(1)} %reshape.87.refs_0_, f32[64]{0:T(128)S(1)} %reshape.90.refs_1_, f32[4,2,128,128]{3,2,1,0:T(8,128)S(1)} %copy-done.1, f32[4,2,128,128]{3,2,1,0:T(8,128)S(1)} %get-tuple-element.16.refs_3_.refs_8_, f32[4,2,128,128]{3,2,1,0:T(8,128)S(1)} %broadcast_select_fusion.3.refs_4_, ...), custom_call_target="tpu_custom_call" | custom-call | flops 402653184 | bytes 3145728 | tf_op jit(solution)/shard_map/pallas_call | solution.py:89
  (26 shorter events, 0.2 us)
Async XLA Ops:
  0.0 11.9 %copy-start = (s32[4,4]{1,0:T(4,128)S(1)}, s32[4,4]{1,0:T(4,128)}, u32[]{:S(2)}) copy-start(s32[4,4]{1,0:T(4,128)} %param.5) | copy-start | bytes 196
  0.0 19.2 %collective-permute-start.3 = (f32[4,2,128,128]{3,2,1,0:T(8,128)}, f32[4,2,128,128]{3,2,1,0:T(8,128)S(1)}, u32[]{:S(2)}, u32[]{:S(2)}) collective-permute-start(f32[4,2,128,128]{3,2,1,0:T(8,128)} %refs_2_.3), channel_id=1, source_target_pairs={{1,0},{0,1},{30,2},{31,3},{5,4},{4,5},{2,6},{3,7},{9,8},{8,9},{6,1... | collective-permute-start | bytes 1572872 | tf_op jit(solution)/shard_map/ppermute | solution.py:113
  2.9 19.7 %collective-permute-start.4 = (f32[4,2,128,128]{3,2,1,0:T(8,128)}, f32[4,2,128,128]{3,2,1,0:T(8,128)S(1)}, u32[]{:S(2)}, u32[]{:S(2)}) collective-permute-start(f32[4,2,128,128]{3,2,1,0:T(8,128)} %refs_2_.3), channel_id=1, source_target_pairs={{28,0},{29,1},{3,2},{2,3},{0,4},{1,5},{7,6},{6,7},{4,8},{5,9},{11,... | collective-permute-start | bytes 1572872 | tf_op jit(solution)/shard_map/ppermute | solution.py:113
  5.2 10.4 %collective-permute-start.1 = (s32[4,4]{0,1:T(4,128)S(1)}, s32[4,4]{0,1:T(4,128)S(1)}, u32[]{:S(2)}, u32[]{:S(2)}) collective-permute-start(s32[4,4]{0,1:T(4,128)S(1)} %copy.12), channel_id=1, source_target_pairs={{30,0},{31,1},{0,2},{1,3},{2,4},{3,5},{4,6},{5,7},{6,8},{7,9},{8,1... | collective-permute-start | bytes 200 | tf_op jit(solution)/shard_map/ppermute | solution.py:113
  5.2 10.4 %collective-permute-start.2 = (s32[4,4]{0,1:T(4,128)S(1)}, s32[4,4]{0,1:T(4,128)S(1)}, u32[]{:S(2)}, u32[]{:S(2)}) collective-permute-start(s32[4,4]{0,1:T(4,128)S(1)} %copy.12), channel_id=1, source_target_pairs={{2,0},{3,1},{4,2},{5,3},{6,4},{7,5},{8,6},{9,7},{10,8},{11,9},{12,... | collective-permute-start | bytes 200 | tf_op jit(solution)/shard_map/ppermute | solution.py:113
  9.7 8.6 %collective-permute-start = (s32[4,4]{0,1:T(4,128)S(1)}, s32[4,4]{0,1:T(4,128)S(1)}, u32[]{:S(2)}, u32[]{:S(2)}) collective-permute-start(s32[4,4]{0,1:T(4,128)S(1)} %copy.12), channel_id=1, source_target_pairs={{28,0},{29,1},{30,2},{31,3},{0,4},{1,5},{2,6},{3,7},{4,8},{5,9},{6... | collective-permute-start | bytes 200 | tf_op jit(solution)/shard_map/ppermute | solution.py:113
  9.7 0.7 %copy-start.2 = (s32[4,4]{1,0:T(4,128)S(1)}, s32[4,4]{1,0:T(4,128)}, u32[]{:S(2)}) copy-start(s32[4,4]{1,0:T(4,128)} %param.4) | copy-start | bytes 196
  15.6 19.1 %collective-permute-start.8 = (f32[4,2,128,128]{3,2,1,0:T(8,128)}, f32[4,2,128,128]{3,2,1,0:T(8,128)S(1)}, u32[]{:S(2)}, u32[]{:S(2)}) collective-permute-start(f32[4,2,128,128]{3,2,1,0:T(8,128)} %refs_2_.3), channel_id=1, source_target_pairs={{2,0},{3,1},{0,2},{1,3},{6,4},{7,5},{4,6},{5,7},{10,8},{11,9},{8,1... | collective-permute-start | bytes 1572872 | tf_op jit(solution)/shard_map/ppermute | solution.py:113
  19.2 8.3 %collective-permute-start.10 = (f32[4,2,128,128]{3,2,1,0:T(8,128)}, f32[4,2,128,128]{3,2,1,0:T(8,128)S(1)}, u32[]{:S(2)}, u32[]{:S(2)}) collective-permute-start(f32[4,2,128,128]{3,2,1,0:T(8,128)} %refs_2_.3), channel_id=1, source_target_pairs={{4,2},{5,3},{8,6},{9,7},{12,10},{13,11},{16,14},{17,15},{20,18},{2... | collective-permute-start | bytes 1572872 | tf_op jit(solution)/shard_map/ppermute | solution.py:113
  20.8 12.8 %collective-permute-start.9 = (f32[4,2,128,128]{3,2,1,0:T(8,128)S(1)}, f32[4,2,128,128]{3,2,1,0:T(8,128)S(1)}, u32[]{:S(2)}, u32[]{:S(2)}) collective-permute-start(f32[4,2,128,128]{3,2,1,0:T(8,128)S(1)} %collective-permute-done.3), channel_id=1, source_target_pairs={{2,0},{3,1},{0,2},{1,3},{6,4},{7,5},{4,6},{5,7},{10,8},{11,9},{8,1... | collective-permute-start | bytes 1572872 | tf_op jit(solution)/shard_map/ppermute | solution.py:113
  20.9 12.7 %collective-permute-start.6 = (f32[4,2,128,128]{3,2,1,0:T(8,128)S(1)}, f32[4,2,128,128]{3,2,1,0:T(8,128)S(1)}, u32[]{:S(2)}, u32[]{:S(2)}) collective-permute-start(f32[4,2,128,128]{3,2,1,0:T(8,128)S(1)} %collective-permute-done.3), channel_id=1, source_target_pairs={{4,0},{5,1},{3,2},{2,3},{8,4},{9,5},{7,6},{6,7},{12,8},{13,9},{11,... | collective-permute-start | bytes 1572872 | tf_op jit(solution)/shard_map/ppermute | solution.py:113
  22.7 10.9 %collective-permute-start.11 = (f32[4,2,128,128]{3,2,1,0:T(8,128)S(1)}, f32[4,2,128,128]{3,2,1,0:T(8,128)}, u32[]{:S(2)}, u32[]{:S(2)}) collective-permute-start(f32[4,2,128,128]{3,2,1,0:T(8,128)S(1)} %collective-permute-done.4), channel_id=1, source_target_pairs={{2,0},{3,1},{6,4},{7,5},{10,8},{11,9},{14,12},{15,13},{18,16},{19,... | collective-permute-start | bytes 1572872 | tf_op jit(solution)/shard_map/ppermute | solution.py:113
  27.5 11.3 %collective-permute-start.5 = (f32[4,2,128,128]{3,2,1,0:T(8,128)S(1)}, f32[4,2,128,128]{3,2,1,0:T(8,128)S(1)}, u32[]{:S(2)}, u32[]{:S(2)}) collective-permute-start(f32[4,2,128,128]{3,2,1,0:T(8,128)S(1)} %collective-permute-done.4), channel_id=1, source_target_pairs={{1,0},{0,1},{5,4},{4,5},{9,8},{8,9},{13,12},{12,13},{17,16},{16,17... | collective-permute-start | bytes 1572872 | tf_op jit(solution)/shard_map/ppermute | solution.py:113
  31.7 3.1 %copy-start.1 = (f32[4,2,128,128]{3,2,1,0:T(8,128)S(1)}, f32[4,2,128,128]{3,2,1,0:T(8,128)}, u32[]{:S(2)}) copy-start(f32[4,2,128,128]{3,2,1,0:T(8,128)} %refs_2_.3) | copy-start | bytes 1572868
  33.6 5.2 %collective-permute-start.7 = (f32[4,2,128,128]{3,2,1,0:T(8,128)S(1)}, f32[4,2,128,128]{3,2,1,0:T(8,128)S(1)}, u32[]{:S(2)}, u32[]{:S(2)}) collective-permute-start(f32[4,2,128,128]{3,2,1,0:T(8,128)S(1)} %collective-permute-done.6), channel_id=1, source_target_pairs={{2,0},{3,1},{0,2},{1,3},{6,4},{7,5},{4,6},{5,7},{10,8},{11,9},{8,1... | collective-permute-start | bytes 1572872 | tf_op jit(solution)/shard_map/ppermute | solution.py:113
